TPU v7x, 32 devices: a whole 2x2x4 slice. The times are simulated.
32 devices in a mesh: groups: 2 (over y), seq: 4 (over z), tp: 2 (over x), dp: 2 (over core).
Axes of the slice: x: 2, y: 2, z: 4, core: 2. Of those that a mesh axis runs over, the one named last changes fastest.
Arguments:
- byte_rows: bfloat16 [16384, 1024], P(('groups', 'seq', 'dp')), parts along dimension 0, may hold values from -80 to 80
- patch_lengths: int32 [16, 128], P(('groups', 'seq', 'dp')), parts along dimension 0, may hold values from 1 to 32, 1024 in all within a row
- patch_owner: int32 [2048, 1], P(('groups', 'seq', 'dp')), parts along dimension 0, may hold values from 0 to 7; in each aligned block of 128 rows (0 to 127, 128 to 255, ...) at most 32 rows name the same one
- patch_stream: bfloat16 [4096, 4096], P(('groups', 'seq', 'dp'), 'tp'), parts along dimension 0, may hold values from -80 to 80
- w_in: bfloat16 [1024, 4096], P(('seq', 'dp'), 'tp'), may hold values from -0.1875 to 0.1875
- norm_gain: float32 [4096], P('tp'), may hold values from 0.1 to 1.9
- w_kv: bfloat16 [2, 4096, 1024], P(None, 'tp', ('seq', 'dp')), may hold values from -0.09375 to 0.09375
- w_query: bfloat16 [1024, 1024], P(None, 'tp'), may hold values from -0.1875 to 0.1875
- w_out: bfloat16 [1024, 1024], P(None, 'tp'), may hold values from -0.1875 to 0.1875
Outputs:
- decoded: bfloat16 [16384, 1024], P(('groups', 'seq', 'dp'), 'tp'), parts along dimension 0
There are 2 independent parts, one for each index of `groups`. A program takes and returns all parts, laid end to end along the dimension named above; an argument that names none is the same for every part. Nothing has to cross between parts.
Inputs may be any that keep to these rules, and one draw needn't show every extreme that they name: `patch_lengths`: row b gives the lengths of the 128 patches that begin and end inside byte block b; every row sums to 1024. `patch_owner`: owners are numbered in the order of seq then dp. Among the 128 patches of one byte block no owner appears more than 32 times, a bound that some block reaches; every owner has some patch.
All inputs are finite; a program needn't handle non-finite values.
Results may differ from a plain program's by a relative error of at most 0.0051.
Values may be sent and summed in bfloat16 or wider, within the bound.
A program may use at most 64 MiB of HBM per device.

v0:
```python
import math

import jax
import jax.numpy as jnp
from jax import lax
from jax.sharding import PartitionSpec as P

D = 4096
HEAD_DIM = 64
WIN = 8


def shifted(block, axis, distance):
    devices = range(lax.axis_size(axis))
    route = [(i - distance, i) for i in devices if i - distance in devices]
    return lax.ppermute(block, axis, route)


def local(
    byte_rows, patch_lengths, patch_owner, patch_stream, w_in, norm_gain, w_kv, w_query, w_out
):
    sources = lax.axis_size(("seq", "dp"))
    lens = patch_lengths[0]
    count = lens.shape[0]
    byte_count = byte_rows.shape[0]
    slots = patch_stream.shape[0]
    cap = slots // sources
    quarter = w_query.shape[1]
    ends = jnp.cumsum(lens)
    starts = ends - lens
    places = jnp.arange(byte_count, dtype=jnp.int32)
    members = ((places[None, :] >= starts[:, None]) & (places[None, :] < ends[:, None])).astype(
        jnp.bfloat16
    )
    sums = jnp.dot(members, byte_rows, preferred_element_type=jnp.float32)
    pooled = (sums / lens[:, None].astype(jnp.float32)).astype(jnp.bfloat16)
    owners = patch_owner[:, 0]
    match = (owners[:, None] == jnp.arange(sources, dtype=jnp.int32)[None, :]).astype(jnp.int32)
    ranking = jnp.sum(jnp.cumsum(match, axis=0) * match, axis=1) - 1
    targets = owners * cap + ranking
    dispatch = (jnp.arange(slots, dtype=jnp.int32)[:, None] == targets[None, :]).astype(
        jnp.bfloat16
    )
    outgoing = jnp.dot(dispatch, pooled, preferred_element_type=jnp.float32).astype(jnp.bfloat16)
    outgoing = outgoing.reshape(sources, cap, outgoing.shape[1])
    arrived = lax.all_to_all(outgoing, ("seq", "dp"), split_axis=0, concat_axis=0, tiled=True)
    inputs = arrived.reshape(slots, arrived.shape[2])
    mixed = jnp.dot(
        inputs,
        lax.all_gather(w_in, ("seq", "dp"), axis=0, tiled=True),
        preferred_element_type=jnp.float32,
    )
    mixed = mixed + patch_stream.astype(jnp.float32)
    squares = lax.psum(jnp.sum(mixed * mixed, axis=1), "tp")
    normed = (mixed * lax.rsqrt(squares / D + 1e-06)[:, None] * norm_gain[None, :]).astype(
        jnp.bfloat16
    )
    partial_kv = jnp.einsum(
        "sd,kdc->skc",
        normed,
        lax.all_gather(w_kv, ("seq", "dp"), axis=2, tiled=True),
        preferred_element_type=jnp.float32,
    )
    kv_slots = lax.psum_scatter(partial_kv, "tp", scatter_dimension=2, tiled=True).astype(
        jnp.bfloat16
    )
    returned = lax.all_to_all(
        kv_slots.reshape(sources, cap, 2, quarter),
        ("seq", "dp"),
        split_axis=0,
        concat_axis=0,
        tiled=True,
    )
    kv_patch = jnp.einsum(
        "sp,skc->pkc",
        dispatch,
        returned.reshape(slots, 2, quarter),
        preferred_element_type=jnp.float32,
    ).astype(jnp.bfloat16)
    prior = shifted(kv_patch[count - (WIN - 1) :], ("seq", "dp"), 1)
    window_kv = jnp.concatenate([prior, kv_patch], axis=0)
    query = jnp.dot(byte_rows, w_query, preferred_element_type=jnp.float32).astype(jnp.bfloat16)
    heads = quarter // HEAD_DIM
    mine = jnp.sum((ends[None, :] <= places[:, None]).astype(jnp.int32), axis=1)
    key_index = jnp.arange(count + WIN - 1, dtype=jnp.int32) - (WIN - 1)
    first_block = lax.axis_index(("seq", "dp")) == 0
    allowed = (key_index[None, :] <= mine[:, None]) & (key_index[None, :] > mine[:, None] - WIN)
    allowed = allowed & ((key_index[None, :] >= 0) | jnp.logical_not(first_block))
    queries = query.reshape(byte_count, heads, HEAD_DIM)
    keys = window_kv[:, 0].reshape(-1, heads, HEAD_DIM)
    values = window_kv[:, 1].reshape(-1, heads, HEAD_DIM)
    scores = jnp.einsum("ihe,khe->hik", queries, keys, preferred_element_type=jnp.float32) * (
        1.0 / math.sqrt(HEAD_DIM)
    )
    scores = jnp.where(allowed[None, :, :], scores, -1e30)
    top = jnp.max(scores, axis=-1, keepdims=True)
    expo = jnp.exp(scores - top)
    weights = (expo / jnp.sum(expo, axis=-1, keepdims=True)).astype(jnp.bfloat16)
    attended = jnp.einsum("hik,khe->ihe", weights, values, preferred_element_type=jnp.float32)
    attended = attended.astype(jnp.bfloat16).reshape(byte_count, quarter)
    projected = jnp.dot(
        lax.all_gather(attended, "tp", axis=1, tiled=True),
        w_out,
        preferred_element_type=jnp.float32,
    )
    residual = lax.dynamic_slice_in_dim(byte_rows, lax.axis_index("tp") * quarter, quarter, 1)
    return (residual.astype(jnp.float32) + projected).astype(jnp.bfloat16)


def solution(mesh):
    return jax.shard_map(
        local,
        mesh=mesh,
        in_specs=(
            P(("groups", "seq", "dp"), None),
            P(("groups", "seq", "dp"), None),
            P(("groups", "seq", "dp"), None),
            P(("groups", "seq", "dp"), "tp"),
            P(("seq", "dp"), "tp"),
            P("tp"),
            P(None, "tp", ("seq", "dp")),
            P(None, "tp"),
            P(None, "tp"),
        ),
        out_specs=P(("groups", "seq", "dp"), "tp"),
        check_vma=False,
    )
```

profile of v0, /device:TPU:0, one launch (start us, length us, event | category | flops | bytes accessed | tf_op | source)
XLA Modules:
  0.0 268.2 jit_solution(7930722522284724898)
XLA Ops:
  6.5 0.7 all-gather.4.cloned.1.call-update
  7.3 0.7 all-gather.6.cloned.1.call-update
  8.1 0.8 copy.21
  9.1 0.7 fusion.28
  10.0 0.8 select_reduce_fusion
  10.9 2.4 convolution_convert_fusion.1
  13.3 35.5 %all_to_all.10 = bf16[8,32,1024]{2,1,0:T(8,128)(2,1)S(1)} all-to-all(bf16[8,32,1024]{2,1,0:T(8,128)(2,1)S(1)} %bitcast.40), channel_id=1, replica_groups=mesh['groups'=2,'seq'=4,'tp'=2,'dp'=2] {'seq','dp'}, dimensions={0} | all-to-all | bytes 1048576 | tf_op jit(solution)/shard_map/all_to_all | solution.py:46
  48.8 21.1 %all-gather.4.cloned.1.call-done = bf16[1024,2048]{1,0:T(8,128)(2,1)} async-done(((bf16[128,2048]{1,0:T(8,128)(2,1)}), bf16[1024,2048]{1,0:T(8,128)(2,1)}) %all-gather.4.cloned.1.call-update) | async-done | bytes 4194320 | tf_op jit(solution)/shard_map/all_gather | solution.py:50
  70.0 4.9 %multiply_reduce_fusion = (f32[256]{0:T(256)S(1)}, f32[256,2048]{1,0:T(8,128)}) fusion(bf16[256,2048]{1,0:T(8,128)(2,1)S(1)} %copy-done.3, bf16[256,1024]{1,0:T(8,128)(2,1)S(1)} %bitcast.39, bf16[1024,2048]{1,0:T(8,128)(2,1)} %all-gather.4.cloned.1.call-done), kind=kOutput, calls=%fused_computation.12 | convolution fusion | flops 1075838720 | bytes 7865344 | tf_op jit(solution)/shard_map/dot_general | solution.py:48
  74.8 4.9 %psum.7 = f32[256]{0:T(256)S(1)} all-reduce(f32[256]{0:T(256)S(1)} %get-tuple-element.7), channel_id=1, replica_groups=mesh['groups'=2,'seq'=4,'tp'=2,'dp'=2] {'tp'}, use_global_device_ids=true, to_apply=%region_4.5 | all-reduce | flops 256 | bytes 2048 | tf_op jit(solution)/shard_map/psum | solution.py:54
  79.8 72.9 %all-gather.6.cloned.1.call-done = bf16[2,2048,1024]{2,1,0:T(8,128)(2,1)} async-done(((bf16[2,2048,128]{2,1,0:T(8,128)(2,1)}), bf16[2,2048,1024]{2,1,0:T(8,128)(2,1)}) %all-gather.6.cloned.1.call-update) | async-done | bytes 8388624 | tf_op jit(solution)/shard_map/all_gather | solution.py:61
  152.7 7.8 %fusion.9 = f32[256,2,1024]{2,0,1:T(8,128)} fusion(bf16[2,2048,1024]{2,1,0:T(8,128)(2,1)} %all-gather.6.cloned.1.call-done, f32[256,2048]{1,0:T(8,128)} %get-tuple-element.8, f32[2048]{0:T(1024)S(1)} %copy-done.5, f32[256]{0:T(256)S(1)} %add_rsqrt_fusion), kind=kOutput, calls=%fused_computation.20 | convolution fusion | flops 2149056512 | bytes 12592128 | tf_op jit(solution)/shard_map/sd,kdc->skc/dot_general | solution.py:58
  160.6 30.1 %reduce-scatter.2.cloned.1.call-done = f32[256,2,512]{2,0,1:T(8,128)} async-done(((f32[256,2,1024]{2,0,1:T(8,128)}), f32[256,2,512]{2,0,1:T(8,128)}) %reduce-scatter.2.cloned.1.call-update) | async-done | bytes 1048592 | tf_op jit(solution)/shard_map/reduce_scatter | solution.py:64
  190.7 1.3 convert_element_type.59
  192.0 0.8 copy.22
  192.8 4.6 %all-to-all-start.1 = ((bf16[8,32,2,512]{3,1,2,0:T(8,128)(2,1)}), bf16[8,32,2,512]{3,1,2,0:T(8,128)(2,1)S(1)}, u32[]{:S(2)}, u32[]{:S(2)}) async-start(bf16[8,32,2,512]{3,1,2,0:T(8,128)(2,1)} %copy.22), calls=%async_computation.2 | async-start | bytes 1048576 | tf_op jit(solution)/shard_map/all_to_all | solution.py:67
  197.8 2.9 %convolution_convert_fusion = bf16[1024,512]{0,1:T(8,128)(2,1)S(1)} fusion(bf16[1024,1024]{1,0:T(8,128)(2,1)} %param.9, bf16[1024,512]{1,0:T(8,128)(2,1)S(1)} %copy-done), kind=kOutput, calls=%fused_computation.14 | convolution fusion | flops 1074266112 | bytes 4194304 | tf_op jit(solution)/shard_map/dot_general | solution.py:82
  200.7 12.2 %all-to-all-done.1 = bf16[8,32,2,512]{3,1,2,0:T(8,128)(2,1)S(1)} async-done(((bf16[8,32,2,512]{3,1,2,0:T(8,128)(2,1)}), bf16[8,32,2,512]{3,1,2,0:T(8,128)(2,1)S(1)}, u32[]{:S(2)}, u32[]{:S(2)}) %all-to-all-start.1) | async-done | bytes 524320 | tf_op jit(solution)/shard_map/all_to_all | solution.py:67
  213.2 1.5 collective-permute-start
  214.9 0.6 collective-permute-done
  215.9 3.9 %fusion.31 = (f32[8,1024]{1,0:T(8,128)S(1)}, f32[8,1024,135]{1,2,0:T(8,128)}) fusion(pred[1024,135]{0,1:T(8,128)(4,1)S(1)} %and_and_fusion, bf16[1024,8,64]{0,2,1:T(8,128)(2,1)S(1)} %bitcast.46, bf16[135,8,64]{0,2,1:T(8,128)(2,1)S(1)} %bitcast.41), kind=kOutput, calls=%fused_computation.53 | convolution fusion | flops 145981568 | bytes 5781504 | tf_op jit(solution)/shard_map/sub | solution.py:97
  219.8 3.9 %fusion.6 = bf16[8,64,1024]{2,1,0:T(8,128)(2,1)} fusion(bf16[135,8,64]{0,2,1:T(8,128)(2,1)S(1)} %bitcast.42, f32[8,1024,135]{1,2,0:T(8,128)} %get-tuple-element.10, f32[8,1024]{1,0:T(8,128)S(1)} %get-tuple-element.9), kind=kOutput, calls=%fused_computation.13 | convolution fusion | flops 144293888 | bytes 5643264 | tf_op jit(solution)/shard_map/hik,khe->ihe/dot_general | solution.py:99
  223.7 33.9 %all-gather.8.cloned.1.call-done = bf16[1024,1024]{0,1:T(8,128)(2,1)} async-done(((bf16[1024,512]{0,1:T(8,128)(2,1)}), bf16[1024,1024]{0,1:T(8,128)(2,1)}) %all-gather.8.cloned.1.call-update) | async-done | bytes 2097168 | tf_op jit(solution)/shard_map/all_gather | solution.py:102
  257.5 4.1 %add_convert_fusion = bf16[1024,512]{1,0:T(8,128)(2,1)} fusion(bf16[1024,1024]{0,1:T(8,128)(2,1)} %all-gather.8.cloned.1.call-done, bf16[1024,512]{1,0:T(8,128)(2,1)S(1)} %copy-done.4, bf16[1024,1024]{1,0:T(8,128)(2,1)} %param.9, s32[]{:T(128)S(6)} %select_n.7), kind=kOutput, calls=%fused_computation.10 | convolution fusion | flops 1075314688 | bytes 5242884 | tf_op jit(solution)/shard_map/dot_general | solution.py:101
  (35 shorter events, 1.7 us)
Async XLA Ops:
  6.5 191.2 %copy-start = (bf16[1024,512]{1,0:T(8,128)(2,1)S(1)}, bf16[1024,512]{1,0:T(8,128)(2,1)}, u32[]{:S(2)}) copy-start(bf16[1024,512]{1,0:T(8,128)(2,1)} %param.16) | copy-start | bytes 3145732
  6.5 4.3 %copy-start.2 = (s32[1,128]{1,0:T(1,128)S(1)}, s32[1,128]{1,0:T(1,128)}, u32[]{:S(2)}) copy-start(s32[1,128]{1,0:T(1,128)} %param.10) | copy-start | bytes 1540
  6.5 4.3 %copy-start.1 = (s32[128,1]{0,1:T(1,128)S(1)}, s32[128,1]{0,1:T(1,128)}, u32[]{:S(2)}) copy-start(s32[128,1]{0,1:T(1,128)} %param.11) | copy-start | bytes 1540
  6.5 63.4 %all-gather.4.cloned.1.call-start = ((), (), s32[]{:S(2)}) async-start(), calls=%async_computation.3 | async-start | bytes 4718592 | tf_op jit(solution)/shard_map/all_gather | solution.py:50
  7.3 145.4 %all-gather.6.cloned.1.call-start = ((), (), s32[]{:S(2)}) async-start(), calls=%async_computation.4 | async-start | bytes 9437184 | tf_op jit(solution)/shard_map/all_gather | solution.py:61
  8.0 182.7 %reduce-scatter.2.cloned.1.call-start = ((), (), s32[]{:S(2)}) async-start(), calls=%async_computation.5 | async-start | bytes 3145728 | tf_op jit(solution)/shard_map/reduce_scatter | solution.py:64
  10.9 59.0 %copy-start.3 = (bf16[256,2048]{1,0:T(8,128)(2,1)S(1)}, bf16[256,2048]{1,0:T(8,128)(2,1)}, u32[]{:S(2)}) copy-start(bf16[256,2048]{1,0:T(8,128)(2,1)} %param.12) | copy-start | bytes 3145732
  69.9 82.8 %copy-start.5 = (f32[2048]{0:T(1024)S(1)}, f32[2048]{0:T(1024)}, u32[]{:S(2)}) copy-start(f32[2048]{0:T(1024)} %param.14) | copy-start | bytes 24580
  192.8 20.0 %all-to-all-start.1 = ((bf16[8,32,2,512]{3,1,2,0:T(8,128)(2,1)}), bf16[8,32,2,512]{3,1,2,0:T(8,128)(2,1)S(1)}, u32[]{:S(2)}, u32[]{:S(2)}) async-start(bf16[8,32,2,512]{3,1,2,0:T(8,128)(2,1)} %copy.22), calls=%async_computation.2 | async-start | bytes 1048576 | tf_op jit(solution)/shard_map/all_to_all | solution.py:67
  197.5 60.1 %all-gather.8.cloned.1.call-start = ((), (), s32[]{:S(2)}) async-start(), calls=%async_computation.6 | async-start | bytes 3145728 | tf_op jit(solution)/shard_map/all_gather | solution.py:102
  213.2 2.4 collective-permute-start
  219.8 37.8 %copy-start.4 = (bf16[1024,512]{1,0:T(8,128)(2,1)S(1)}, bf16[1024,512]{1,0:T(8,128)(2,1)}, u32[]{:S(2)}) copy-start(bf16[1024,512]{1,0:T(8,128)(2,1)} %param.17) | copy-start | bytes 3145732
Sparse Core Ops, SparseCore 0:
  9.0 60.9 all-gather.3
  71.5 81.1 all-gather.5
  160.7 29.9 reduce-scatter.1
  223.8 33.7 all-gather.7
where the time goes:
time: 269 us; the launch traced here: 268 us
  waiting for transfers between devices  172 us (64%)
  blocking collectives  40.4 us (15%)
  matrix products  30.1 us (11%)
  between operations  13.3 us (5%)
  starting transfers between devices  6.28 us (2%)
  other arithmetic  3.82 us (1%)
    all_gather x1, waiting for transfers between devices, local(): lax.all_gather(w_kv, ('seq', 'dp'), axis=2, tiled=True)  72.9 us
    all_to_all x1, blocking collectives, local(): lax.all_to_all(outgoing, ('seq', 'dp'), split_axis=0, concat_axis=0, tile...  35.5 us
    all_gather x1, waiting for transfers between devices, local(): lax.all_gather(attended, 'tp', axis=1, tiled=True)  33.9 us
    reduce_scatter x1, waiting for transfers between devices, local(): lax.psum_scatter(partial_kv, 'tp', scatter_dimension=2, tiled=True)  30.1 us
    all_gather x1, waiting for transfers between devices, local(): lax.all_gather(w_in, ('seq', 'dp'), axis=0, tiled=True)  21.1 us
    all_to_all x1, waiting for transfers between devices, local(): lax.all_to_all(kv_slots.reshape(sources, cap, 2, quarter), ('seq', 'dp'),...  12.2 us
    dot_general x1, matrix products, local(): jnp.einsum('sd,kdc->skc', normed, lax.all_gather(w_kv, ('seq', 'dp'), axi...  7.81 us
  transfers between devices with their start and end apart: 6, of which 6 were waited for; matrix products, arithmetic and copies ran while one was open for 5% of the time, Pallas kernels for 0%

commit v1 on v0

--- a/solution.py
+++ b/solution.py
@@ -1,8 +1,11 @@
+import functools
 import math
 
 import jax
 import jax.numpy as jnp
 from jax import lax
+from jax.experimental import pallas as pl
+from jax.experimental.pallas import tpu as pltpu
 from jax.sharding import PartitionSpec as P
 
 D = 4096
@@ -107,9 +110,425 @@
     return (residual.astype(jnp.float32) + projected).astype(jnp.bfloat16)
 
 
+MESH = pl.DeviceIdType.MESH
+HALO = 16
+ROWS = 128
+bf16, f32 = jnp.bfloat16, jnp.float32
+
+
+def iota(shape, axis):
+    return lax.broadcasted_iota(jnp.int32, shape, axis)
+
+
+def fused_kernel(
+    n_seq,
+    rows_ref, lens_ref, own_col_ref, own_row_ref, stream_ref, w_in_ref, gain_ref, w_kv_ref,
+    w_query_ref, w_out_ref, out_ref,
+    win, wkv, arr, br, wq, wo, pooled, mixed, nrm, hs_out, hs_in, part, part_out, part_in,
+    kv, sq, sq_in, query, att, y_out,
+    recv, send_r, send_l, send_y, send_c, local_sem, st_send, st_recv, x_send, x_recv,
+    xc_send, xc_recv, h_send, h_recv, p_send, p_recv, y_send, y_recv,
+):
+    g, s = lax.axis_index("groups"), lax.axis_index("seq")
+    t, d = lax.axis_index("tp"), lax.axis_index("dp")
+    n = n_seq * 2
+    me = s * 2 + d
+    count = own_col_ref.shape[0]
+    byte_count, dl = rows_ref.shape
+    half = byte_count // 2
+    depth, width = w_in_ref.shape
+    cap = stream_ref.shape[0] // n
+    cols = w_query_ref.shape[1]
+    hd = depth // 2
+    hw = width // 2
+    y_peer, c_peer, x_peer = {"groups": 1 - g}, {"dp": 1 - d}, {"tp": 1 - t}
+
+    barrier = pltpu.get_barrier_semaphore()
+
+    def other(i):
+        b = lax.rem(me + i, n)
+        return b, {"seq": b // 2, "dp": lax.rem(b, 2)}
+
+    for i in range(1, n):
+        pl.semaphore_signal(barrier, inc=1, device_id=other(i)[1], device_id_type=MESH)
+    pl.semaphore_signal(barrier, inc=1, device_id=y_peer, device_id_type=MESH)
+    pl.semaphore_signal(barrier, inc=1, device_id=x_peer, device_id_type=MESH)
+
+    local = []
+
+    def bring(src, dst):
+        copy = pltpu.make_async_copy(src, dst, local_sem.at[len(local)])
+        copy.start()
+        local.append(copy)
+
+    bring(rows_ref, br)
+    bring(stream_ref.at[pl.ds(pl.multiple_of(me * cap, cap), cap)], arr.at[pl.ds(pl.multiple_of(me * cap, cap), cap)])
+    bring(w_query_ref, wq.at[t])
+    bring(w_out_ref, wo.at[t])
+    bring(w_in_ref, win.at[pl.ds(pl.multiple_of(me * depth, depth), depth)])
+    bring(w_kv_ref, wkv.at[me])
+    pl.semaphore_wait(barrier, n + 1)
+
+    def remote(src, dst, send, arrive, where):
+        return pltpu.make_async_remote_copy(
+            src_ref=src, dst_ref=dst, send_sem=send, recv_sem=arrive, device_id=where, device_id_type=MESH
+        )
+
+    def held(kind, slot, h):
+        if kind == 0:
+            return win.at[pl.ds(pl.multiple_of(slot * depth + h * hd, hd), hd)]
+        return wkv.at[slot, h, pl.ds((kind - 1) * hw, hw)]
+
+    def own(kind, h):
+        if kind == 0:
+            return w_in_ref.at[pl.ds(pl.multiple_of(h * hd, hd), hd)]
+        return w_kv_ref.at[h, pl.ds((kind - 1) * hw, hw)]
+
+    def piece(kind, z, h, send, where, mine=False, core=None):
+        slot = z * 2 + (d if core is None else core)
+        dst = held(kind, slot, h)
+        return remote(own(kind, h) if mine else dst, dst, send, recv.at[kind, slot, h], where)
+
+    def right(kind, z, mine=False):
+        return piece(kind, z, g, send_r.at[kind, z], {"seq": jnp.minimum(s + 1, n_seq - 1)}, mine)
+
+    def left(kind, z, mine=False):
+        return piece(kind, z, g, send_l.at[kind, z], {"seq": jnp.maximum(s - 1, 0)}, mine)
+
+    def across(kind, z):
+        return piece(kind, z, g, send_y.at[kind, z], y_peer)
+
+    def core(kind, z, h, mine=False):
+        return piece(kind, z, h, send_c.at[kind, z, h], c_peer, mine)
+
+    def ends_of_line(kind):
+        pl.when(s + 1 < n_seq)(lambda: right(kind, s, True).start())
+        pl.when(s > 0)(lambda: left(kind, s, True).start())
+
+    def each(k, fn):
+        pl.when(s - k >= 0)(lambda: fn(s - k, True))
+        pl.when(s + k < n_seq)(lambda: fn(s + k, False))
+
+    def arrive(kind, k):
+        def one(z, from_left):
+            piece(kind, z, g, send_y.at[kind, z], y_peer).wait_recv()
+            if from_left:
+                pl.when(s + 1 < n_seq)(lambda: right(kind, z).start())
+            else:
+                pl.when(s > 0)(lambda: left(kind, z).start())
+            across(kind, z).start()
+            core(kind, z, g).start()
+        each(k, one)
+
+    def arrive_y(kind, k):
+        def one(z, _):
+            piece(kind, z, 1 - g, send_y.at[kind, z], y_peer).wait_recv()
+            core(kind, z, 1 - g).start()
+        each(k, one)
+
+    def arrive_c(kind, k):
+        def one(z, _=None):
+            for h in range(2):
+                piece(kind, z, h, send_c.at[kind, z, h], c_peer, core=1 - d).wait_recv()
+        one(s) if k == 0 else each(k, one)
+
+    ends_of_line(0)
+
+    def stream_copy(i):
+        b, where = other(i)
+        src = stream_ref.at[pl.ds(pl.multiple_of(b * cap, cap), cap)]
+        dst = arr.at[pl.ds(pl.multiple_of(me * cap, cap), cap)]
+        return remote(src, dst, st_send.at[i], st_recv.at[i], where)
+
+    for i in range(1, n):
+        stream_copy(i).start()
+    dh = dl // 2
+    mine_rows = pl.ds(pl.multiple_of(d * dh, dh), dh)
+
+    def x_copy(i):
+        src, dst = ((w_query_ref, wq), (w_out_ref, wo))[i]
+        return remote(src.at[mine_rows], dst.at[t, mine_rows], x_send.at[i], x_recv.at[i], x_peer)
+
+    def xc_copy(i):
+        dst = (wq, wo)[i].at[1 - t, mine_rows]
+        return remote(dst, dst, xc_send.at[i], xc_recv.at[i], c_peer)
+
+    x_copy(0).start()
+    x_copy(1).start()
+    for kind in range(3):
+        for h in range(2):
+            core(kind, s, h, True).start()
+    ends_of_line(1)
+    ends_of_line(2)
+
+    local[0].wait()
+    lens_row = lens_ref[...]
+    tri = iota((count, count), 1) <= iota((count, count), 0)
+    ends_col = jnp.sum(jnp.where(tri, lens_row, 0).astype(f32), axis=1, keepdims=True)
+    lens_col = jnp.sum(
+        jnp.where(iota((count, count), 0) == iota((count, count), 1), lens_row, 0).astype(f32), axis=1, keepdims=True
+    )
+    places = iota((count, byte_count), 1).astype(f32)
+    members = jnp.where((places >= ends_col - lens_col) & (places < ends_col), 1.0, 0.0).astype(bf16)
+    sums = jnp.dot(members, br[...], preferred_element_type=f32)
+    pooled[pl.ds(0, count)] = (sums / lens_col).astype(bf16)
+    _, following = other(1)
+    halo_pooled = remote(
+        pooled.at[pl.ds(count - HALO, HALO)], pooled.at[pl.ds(count, HALO)], h_send.at[0], h_recv.at[0], following
+    )
+    halo_pooled.start()
+
+    arrive(0, 1)
+    x_copy(0).wait_recv()
+    xc_copy(0).start()
+    x_copy(1).wait_recv()
+    xc_copy(1).start()
+    arrive(0, 2)
+    local[2].wait()
+    xc_copy(0).wait_recv()
+    my_bytes = pl.ds(pl.multiple_of(t * half, half), half)
+    for part_t in range(2):
+        query[:, part_t * cols:(part_t + 1) * cols] = jnp.dot(
+            br[my_bytes, :], wq[part_t], preferred_element_type=f32
+        ).astype(bf16)
+    arrive_y(0, 1)
+    arrive(0, 3)
+
+    for i in range(1, n):
+        stream_copy(i).wait_recv()
+    local[1].wait()
+    owner = own_col_ref[...]
+    same = (owner == own_row_ref[...]) & (iota((count, count), 1) < iota((count, count), 0))
+    ranking = jnp.sum(jnp.where(same, 1.0, 0.0), axis=1, keepdims=True)
+    target = owner.astype(f32) * cap + ranking
+    pick = jnp.where(iota((count, n * cap), 1).astype(f32) == target, 1.0, 0.0).astype(bf16)
+    mixed[pl.ds(0, count)] = jnp.dot(pick, arr[...], preferred_element_type=f32)
+    hs_out[...] = mixed[pl.ds(count - HALO, HALO)].astype(bf16)
+    halo_stream = remote(hs_out, hs_in, h_send.at[1], h_recv.at[1], following)
+    halo_stream.start()
+    arrive(1, 1)
+    arrive_y(0, 2)
+    arrive(2, 1)
+    arrive_y(0, 3)
+    for k in range(n_seq):
+        arrive_c(0, k)
+    local[4].wait()
+    halo_pooled.wait_recv()
+    halo_stream.wait_recv()
+    mixed[pl.ds(count, HALO)] = hs_in[...].astype(f32)
+    step = 512
+    total = jnp.zeros((count + HALO, 128), f32)
+    for c in range(width // step):
+        at = pl.ds(c * step, step)
+        now = mixed[:, at] + jnp.dot(pooled[...], win[:, at], preferred_element_type=f32)
+        nrm[:, at] = (now * gain_ref[:, at]).astype(bf16)
+        for j in range(step // 128):
+            lane = now[:, j * 128:(j + 1) * 128]
+            total = total + lane * lane
+    sq[...] = total
+    sq_copy = remote(sq, sq_in, p_send.at[n], p_recv.at[n], x_peer)
+    sq_copy.start()
+
+    def part_copy(slot):
+        return remote(part_out.at[slot], part_in.at[slot], p_send.at[slot], p_recv.at[slot], x_peer)
+
+    def project(z, _=None):
+        for c in range(2):
+            slot = z * 2 + c
+            for h in range(2):
+                val = jnp.dot(nrm[...], wkv[slot, h], preferred_element_type=f32)
+                part[slot, :, pl.ds(h * 128, 128)] = val
+                part_out[slot, :, pl.ds(h * 128, 128)] = val.astype(bf16)
+            part_copy(slot).start()
+
+    arrive(1, 2)
+    arrive_y(1, 1)
+    arrive(2, 2)
+    arrive_y(2, 1)
+    local[5].wait()
+    arrive_c(1, 0)
+    arrive_c(2, 0)
+    project(s)
+    arrive(1, 3)
+    arrive_y(1, 2)
+    arrive(2, 3)
+    arrive_c(1, 1)
+    arrive_c(2, 1)
+    each(1, project)
+    arrive_y(2, 2)
+    arrive_y(1, 3)
+    arrive_c(1, 2)
+    arrive_c(2, 2)
+    each(2, project)
+    arrive_y(2, 3)
+    arrive_c(1, 3)
+    arrive_c(2, 3)
+    each(3, project)
+
+    ends_row = jnp.dot(
+        jnp.broadcast_to(lens_row.astype(f32), (8, count)).astype(bf16),
+        jnp.where(iota((count, count), 0) <= iota((count, count), 1), 1.0, 0.0).astype(bf16),
+        preferred_element_type=f32,
+    )[0:1]
+    sq_copy.wait_recv()
+    square = jnp.sum(sq[...] + sq_in[...], axis=1, keepdims=True)
+    scale = lax.rsqrt(square / D + 1e-06)
+
+    def finish(slot, carry):
+        part_copy(slot).wait_recv()
+        kv[slot] = ((part[slot] + part_in[slot].astype(f32)) * scale).astype(bf16)
+        return carry
+
+    lax.fori_loop(0, n, finish, 0)
+    local[3].wait()
+    xc_copy(1).wait_recv()
+    keys_n = count + HALO
+    key = iota((1, keys_n), 1)
+    key = jnp.where(key < count, key, key - keys_n).astype(f32)
+    first = me == 0
+    low_half = iota((keys_n, 128), 1) < HEAD_DIM
+
+    def y_copy(r):
+        at = pl.ds(pl.multiple_of(t * half + r * ROWS, ROWS), ROWS)
+        return remote(y_out.at[pl.ds(r * ROWS, ROWS)], out_ref.at[at], y_send.at[r], y_recv.at[r], x_peer)
+
+    for r in range(half // ROWS):
+        place = (iota((ROWS, 1), 0) + (t * half + r * ROWS)).astype(f32)
+        patch = jnp.sum(jnp.where(ends_row <= place, 1.0, 0.0), axis=1, keepdims=True)
+        floor = jnp.where(first, jnp.maximum(patch - WIN, -1.0), patch - WIN)
+        bias = jnp.where((key <= patch) & (key > floor), 0.0, -1e30)
+
+        def heads(slot, carry):
+            at = pl.ds(pl.multiple_of(slot * 128, 128), 128)
+            q = query[pl.ds(r * ROWS, ROWS), at]
+            keys, values = kv[slot, :, pl.ds(0, 128)], kv[slot, :, pl.ds(128, 128)]
+            result = jnp.zeros((ROWS, 128), f32)
+            for low in (True, False):
+                pick_head = low_half if low else jnp.logical_not(low_half)
+                kh = jnp.where(pick_head, keys, jnp.zeros_like(keys))
+                vh = jnp.where(pick_head, values, jnp.zeros_like(values))
+                scores = lax.dot_general(q, kh, (((1,), (1,)), ((), ())), preferred_element_type=f32)
+                scores = scores * (1.0 / math.sqrt(HEAD_DIM)) + bias
+                expo = jnp.exp(scores - jnp.max(scores, axis=1, keepdims=True))
+                weights = (expo / jnp.sum(expo, axis=1, keepdims=True)).astype(bf16)
+                result = result + jnp.dot(weights, vh, preferred_element_type=f32)
+            att[pl.ds(r * ROWS, ROWS), at] = result.astype(bf16)
+            return carry
+
+        lax.fori_loop(0, n, heads, 0)
+        at = pl.ds(pl.multiple_of(t * half + r * ROWS, ROWS), ROWS)
+        a = att[pl.ds(r * ROWS, ROWS), :]
+        for who in (1 - t, t):
+            at_cols = pl.ds(pl.multiple_of(who * cols, cols), cols)
+            value = br[at, at_cols].astype(f32) + jnp.dot(a, wo[who], preferred_element_type=f32)
+            if who is t:
+                out_ref[at, :] = value.astype(bf16)
+            else:
+                y_out[pl.ds(r * ROWS, ROWS), :] = value.astype(bf16)
+                y_copy(r).start()
+
+    for r in range(half // ROWS):
+        y_copy(r).wait()
+    for kind in range(3):
+        pl.when(s + 1 < n_seq)(lambda: right(kind, s, True).wait_send())
+        pl.when(s > 0)(lambda: left(kind, s, True).wait_send())
+        for h in range(2):
+            core(kind, s, h, True).wait_send()
+        for k in range(1, n_seq):
+            def sent(z, from_left):
+                if from_left:
+                    pl.when(s + 1 < n_seq)(lambda: right(kind, z).wait_send())
+                else:
+                    pl.when(s > 0)(lambda: left(kind, z).wait_send())
+                across(kind, z).wait_send()
+                core(kind, z, 0).wait_send()
+                core(kind, z, 1).wait_send()
+            each(k, sent)
+    for i in range(1, n):
+        stream_copy(i).wait_send()
+    for i in range(2):
+        x_copy(i).wait_send()
+        xc_copy(i).wait_send()
+    halo_pooled.wait_send()
+    halo_stream.wait_send()
+    sq_copy.wait_send()
+    lax.fori_loop(0, n, lambda slot, carry: (part_copy(slot).wait_send(), carry)[1], 0)
+
+
+def fused(
+    byte_rows, patch_lengths, patch_owner, patch_stream, w_in, norm_gain, w_kv, w_query, w_out
+):
+    n_seq = lax.axis_size("seq")
+    n = n_seq * 2
+    byte_count, dl = byte_rows.shape
+    count = patch_owner.shape[0]
+    depth, width = w_in.shape
+    cols = w_query.shape[1]
+    half = byte_count // 2
+    tall = count + HALO
+    chunks = half // ROWS
+    any_spec, vmem = pl.BlockSpec(memory_space=pl.ANY), pl.BlockSpec(memory_space=pltpu.VMEM)
+    dma = pltpu.SemaphoreType.DMA
+    return pl.pallas_call(
+        functools.partial(fused_kernel, n_seq),
+        out_shape=jax.ShapeDtypeStruct((byte_count, cols), bf16),
+        in_specs=[any_spec, vmem, vmem, vmem, any_spec, any_spec, vmem, any_spec, any_spec, any_spec],
+        out_specs=vmem,
+        scratch_shapes=[
+            pltpu.VMEM((n * depth, width), bf16),
+            pltpu.VMEM((n, 2, width, 128), bf16),
+            pltpu.VMEM(patch_stream.shape, bf16),
+            pltpu.VMEM((byte_count, dl), bf16),
+            pltpu.VMEM((2, dl, cols), bf16),
+            pltpu.VMEM((2, dl, cols), bf16),
+            pltpu.VMEM((tall, dl), bf16),
+            pltpu.VMEM((tall, width), f32),
+            pltpu.VMEM((tall, width), bf16),
+            pltpu.VMEM((HALO, width), bf16),
+            pltpu.VMEM((HALO, width), bf16),
+            pltpu.VMEM((n, tall, 256), f32),
+            pltpu.VMEM((n, tall, 256), bf16),
+            pltpu.VMEM((n, tall, 256), bf16),
+            pltpu.VMEM((n, tall, 256), bf16),
+            pltpu.VMEM((tall, 128), f32),
+            pltpu.VMEM((tall, 128), f32),
+            pltpu.VMEM((half, dl), bf16),
+            pltpu.VMEM((half, dl), bf16),
+            pltpu.VMEM((half, cols), bf16),
+            dma((3, n, 2)),
+            dma((3, n_seq)),
+            dma((3, n_seq)),
+            dma((3, n_seq)),
+            dma((3, n_seq, 2)),
+            dma((6,)),
+            dma((n,)),
+            dma((n,)),
+            dma((2,)),
+            dma((2,)),
+            dma((2,)),
+            dma((2,)),
+            dma((2,)),
+            dma((2,)),
+            dma((n + 1,)),
+            dma((n + 1,)),
+            dma((chunks,)),
+            dma((chunks,)),
+        ],
+        compiler_params=pltpu.CompilerParams(
+            collective_id=0, has_side_effects=True, vmem_limit_bytes=56 * 1024 * 1024
+        ),
+        cost_estimate=pl.CostEstimate(flops=9 * 10**9, bytes_accessed=8 * 10**6, transcendentals=2 * 10**6),
+    )(
+        byte_rows, patch_lengths, patch_owner, patch_owner.reshape(1, count), patch_stream, w_in,
+        norm_gain.reshape(1, width), w_kv, w_query, w_out,
+    )
+
+
 def solution(mesh):
+    sizes = mesh.shape
+    fits = sizes["groups"] == 2 and sizes["tp"] == 2 and sizes["dp"] == 2 and sizes["seq"] == 4
     return jax.shard_map(
-        local,
+        fused if fits else local,
         mesh=mesh,
         in_specs=(
             P(("groups", "seq", "dp"), None),

time: 269 us -> 136 us (0.51)
  waiting for transfers between devices: 172 us -> 0 us
  Pallas kernels: 0 us -> 132 us
  blocking collectives: 40.4 us -> 0 us
  matrix products: 30.1 us -> 0 us
  between operations: 13.3 us -> 0.01 us
  starting transfers between devices: 6.28 us -> 0 us
  other arithmetic: 3.82 us -> 0 us
    pallas_call x0 -> x1, Pallas kernels: none -> 132 us  [fused(): pl.pallas_call(functools.partial(fused_kernel, n_seq), out_shape=jax.Shap...]
    all_gather x3 -> x0, waiting for transfers between devices: 128 us -> none  [the longest x1 72.9 us: local(): lax.all_gather(w_kv, ('seq', 'dp'), axis=2, tiled=True)]
    all_to_all x1 -> x0, blocking collectives: 35.5 us -> none  [local(): lax.all_to_all(outgoing, ('seq', 'dp'), split_axis=0, concat_axis=0, tile...]
    reduce_scatter x1 -> x0, waiting for transfers between devices: 30.1 us -> none  [local(): lax.psum_scatter(partial_kv, 'tp', scatter_dimension=2, tiled=True)]
    dot_general x7 -> x0, matrix products: 26.2 us -> none  [the longest x1 7.81 us: local(): jnp.einsum('sd,kdc->skc', normed, lax.all_gather(w_kv, ('seq', 'dp'), axi...]
    all_to_all x1 -> x0, waiting for transfers between devices: 12.2 us -> none  [local(): lax.all_to_all(kv_slots.reshape(sources, cap, 2, quarter), ('seq', 'dp'),...]
    psum x1 -> x0, blocking collectives: 4.92 us -> none  [local(): squares = lax.psum(jnp.sum(mixed * mixed, axis=1), 'tp')]
    all_to_all x1 -> x0, starting transfers between devices: 4.63 us -> none  [local(): lax.all_to_all(kv_slots.reshape(sources, cap, 2, quarter), ('seq', 'dp'),...]
  transfers between devices with their start and end apart: 6 -> 0, of which waited for: 6 -> 0; matrix products, arithmetic and copies ran while one was open for 5% -> 0% of each run, Pallas kernels for 0% -> 0%
where the time goes in v1:
time: 136 us
  Pallas kernels  132 us (97%)
  local copies, waits for them, and re-layouts  3.65 us (3%)
    pallas_call x1, Pallas kernels, fused(): pl.pallas_call(functools.partial(fused_kernel, n_seq), out_shape=jax.Shap...  132 us
    unnamed x2, local copies, waits for them, and re-layouts  3.65 us

profile of v1, /device:TPU:0, one launch (start us, length us, event | category | flops | bytes accessed | tf_op | source)
XLA Modules:
  0.0 135.8 jit_solution(6512149436032091772)
XLA Ops:
  0.0 1.4 %copy.10.own_col_ref = s32[128,1]{1,0:T(8,128)} copy(s32[128,1]{0,1:T(1,128)} %param.11) | data formatting | bytes 1024 | tf_op args[2]
  1.4 132.2 %shard_map.91 = bf16[1024,512]{1,0:T(8,128)(2,1)} custom-call(bf16[1024,1024]{1,0:T(8,128)(2,1)} %rows_ref.1, s32[1,128]{1,0:T(1,128)} %lens_ref.1, s32[128,1]{1,0:T(8,128)} %copy.10.own_col_ref, s32[1,128]{1,0:T(1,128)} %bitcast.2, bf16[256,2048]{1,0:T(8,128)(2,1)} %stream_ref.1, bf16[128,2048]{1,0:T(8,128)(2,1)} %w_in_ref.1, f32[1,2048]{1,0:T(1,128)} %bitcast.3, ...), custom_call_target="tpu_custom_call" | custom-call | flops 8999999488 | bytes 8000000 | tf_op jit(solution)/shard_map/pallas_call | solution.py:472
  133.6 2.3 %copy.12 = bf16[1024,512]{1,0:T(8,128)(2,1)} copy(bf16[1024,512]{1,0:T(8,128)(2,1)} %shard_map.91) | data formatting | bytes 2097152

commit v2 on v1

--- a/solution.py
+++ b/solution.py
@@ -279,10 +279,13 @@
     halo_pooled.start()
 
     arrive(0, 1)
+    arrive(1, 1)
     x_copy(0).wait_recv()
     xc_copy(0).start()
     x_copy(1).wait_recv()
     xc_copy(1).start()
+    arrive(2, 1)
+    arrive_y(0, 1)
     arrive(0, 2)
     local[2].wait()
     xc_copy(0).wait_recv()
@@ -291,7 +294,11 @@
         query[:, part_t * cols:(part_t + 1) * cols] = jnp.dot(
             br[my_bytes, :], wq[part_t], preferred_element_type=f32
         ).astype(bf16)
-    arrive_y(0, 1)
+    arrive_y(1, 1)
+    arrive(1, 2)
+    arrive_y(2, 1)
+    arrive(2, 2)
+    arrive_y(0, 2)
     arrive(0, 3)
 
     for i in range(1, n):
@@ -306,9 +313,7 @@
     hs_out[...] = mixed[pl.ds(count - HALO, HALO)].astype(bf16)
     halo_stream = remote(hs_out, hs_in, h_send.at[1], h_recv.at[1], following)
     halo_stream.start()
-    arrive(1, 1)
-    arrive_y(0, 2)
-    arrive(2, 1)
+    arrive_y(1, 2)
     arrive_y(0, 3)
     for k in range(n_seq):
         arrive_c(0, k)
@@ -341,26 +346,21 @@
                 part_out[slot, :, pl.ds(h * 128, 128)] = val.astype(bf16)
             part_copy(slot).start()
 
-    arrive(1, 2)
-    arrive_y(1, 1)
-    arrive(2, 2)
-    arrive_y(2, 1)
+    arrive(1, 3)
+    arrive_y(2, 2)
     local[5].wait()
     arrive_c(1, 0)
     arrive_c(2, 0)
     project(s)
-    arrive(1, 3)
-    arrive_y(1, 2)
     arrive(2, 3)
+    arrive_y(1, 3)
     arrive_c(1, 1)
     arrive_c(2, 1)
     each(1, project)
-    arrive_y(2, 2)
-    arrive_y(1, 3)
     arrive_c(1, 2)
     arrive_c(2, 2)
+    arrive_y(2, 3)
     each(2, project)
-    arrive_y(2, 3)
     arrive_c(1, 3)
     arrive_c(2, 3)
     each(3, project)

time: 136 us -> 124 us (0.912)
  Pallas kernels: 132 us -> 120 us
    pallas_call x1, Pallas kernels: 132 us -> 120 us  [fused(): pl.pallas_call(functools.partial(fused_kernel, n_seq), out_shape=jax.Shap...]
where the time goes in v2:
time: 124 us
  Pallas kernels  120 us (97%)
  local copies, waits for them, and re-layouts  3.65 us (3%)
    pallas_call x1, Pallas kernels, fused(): pl.pallas_call(functools.partial(fused_kernel, n_seq), out_shape=jax.Shap...  120 us
    unnamed x2, local copies, waits for them, and re-layouts  3.65 us

profile of v2, /device:TPU:0, one launch (start us, length us, event | category | flops | bytes accessed | tf_op | source)
XLA Modules:
  0.0 123.9 jit_solution(6707604326347999708)
XLA Ops:
  0.0 1.4 %copy.10.own_col_ref = s32[128,1]{1,0:T(8,128)} copy(s32[128,1]{0,1:T(1,128)} %param.11) | data formatting | bytes 1024 | tf_op args[2]
  1.4 120.2 %shard_map.91 = bf16[1024,512]{1,0:T(8,128)(2,1)} custom-call(bf16[1024,1024]{1,0:T(8,128)(2,1)} %rows_ref.1, s32[1,128]{1,0:T(1,128)} %lens_ref.1, s32[128,1]{1,0:T(8,128)} %copy.10.own_col_ref, s32[1,128]{1,0:T(1,128)} %bitcast.2, bf16[256,2048]{1,0:T(8,128)(2,1)} %stream_ref.1, bf16[128,2048]{1,0:T(8,128)(2,1)} %w_in_ref.1, f32[1,2048]{1,0:T(1,128)} %bitcast.3, ...), custom_call_target="tpu_custom_call" | custom-call | flops 8999999488 | bytes 8000000 | tf_op jit(solution)/shard_map/pallas_call | solution.py:472
  121.6 2.3 %copy.12 = bf16[1024,512]{1,0:T(8,128)(2,1)} copy(bf16[1024,512]{1,0:T(8,128)(2,1)} %shard_map.91) | data formatting | bytes 2097152

commit v3 on v2

--- a/solution.py
+++ b/solution.py
@@ -112,7 +112,7 @@
 
 MESH = pl.DeviceIdType.MESH
 HALO = 16
-ROWS = 128
+ROWS = 256
 bf16, f32 = jnp.bfloat16, jnp.float32
 
 
@@ -125,9 +125,9 @@
     rows_ref, lens_ref, own_col_ref, own_row_ref, stream_ref, w_in_ref, gain_ref, w_kv_ref,
     w_query_ref, w_out_ref, out_ref,
     win, wkv, arr, br, wq, wo, pooled, mixed, nrm, hs_out, hs_in, part, part_out, part_in,
-    kv, sq, sq_in, query, att, y_out,
+    kv, sq, sq_in, query, att, bias,
     recv, send_r, send_l, send_y, send_c, local_sem, st_send, st_recv, x_send, x_recv,
-    xc_send, xc_recv, h_send, h_recv, p_send, p_recv, y_send, y_recv,
+    xc_send, xc_recv, h_send, h_recv, p_send, p_recv,
 ):
     g, s = lax.axis_index("groups"), lax.axis_index("seq")
     t, d = lax.axis_index("tp"), lax.axis_index("dp")
@@ -135,7 +135,6 @@
     me = s * 2 + d
     count = own_col_ref.shape[0]
     byte_count, dl = rows_ref.shape
-    half = byte_count // 2
     depth, width = w_in_ref.shape
     cap = stream_ref.shape[0] // n
     cols = w_query_ref.shape[1]
@@ -164,7 +163,7 @@
     bring(rows_ref, br)
     bring(stream_ref.at[pl.ds(pl.multiple_of(me * cap, cap), cap)], arr.at[pl.ds(pl.multiple_of(me * cap, cap), cap)])
     bring(w_query_ref, wq.at[t])
-    bring(w_out_ref, wo.at[t])
+    bring(w_out_ref, wo)
     bring(w_in_ref, win.at[pl.ds(pl.multiple_of(me * depth, depth), depth)])
     bring(w_kv_ref, wkv.at[me])
     pl.semaphore_wait(barrier, n + 1)
@@ -246,15 +245,13 @@
     mine_rows = pl.ds(pl.multiple_of(d * dh, dh), dh)
 
     def x_copy(i):
-        src, dst = ((w_query_ref, wq), (w_out_ref, wo))[i]
-        return remote(src.at[mine_rows], dst.at[t, mine_rows], x_send.at[i], x_recv.at[i], x_peer)
+        return remote(w_query_ref.at[mine_rows], wq.at[t, mine_rows], x_send.at[i], x_recv.at[i], x_peer)
 
     def xc_copy(i):
-        dst = (wq, wo)[i].at[1 - t, mine_rows]
+        dst = wq.at[1 - t, mine_rows]
         return remote(dst, dst, xc_send.at[i], xc_recv.at[i], c_peer)
 
     x_copy(0).start()
-    x_copy(1).start()
     for kind in range(3):
         for h in range(2):
             core(kind, s, h, True).start()
@@ -282,17 +279,14 @@
     arrive(1, 1)
     x_copy(0).wait_recv()
     xc_copy(0).start()
-    x_copy(1).wait_recv()
-    xc_copy(1).start()
     arrive(2, 1)
     arrive_y(0, 1)
     arrive(0, 2)
     local[2].wait()
     xc_copy(0).wait_recv()
-    my_bytes = pl.ds(pl.multiple_of(t * half, half), half)
     for part_t in range(2):
         query[:, part_t * cols:(part_t + 1) * cols] = jnp.dot(
-            br[my_bytes, :], wq[part_t], preferred_element_type=f32
+            br[...], wq[part_t], preferred_element_type=f32
         ).astype(bf16)
     arrive_y(1, 1)
     arrive(1, 2)
@@ -346,6 +340,49 @@
                 part_out[slot, :, pl.ds(h * 128, 128)] = val.astype(bf16)
             part_copy(slot).start()
 
+    ends_row = jnp.dot(
+        jnp.broadcast_to(lens_row.astype(f32), (8, count)).astype(bf16),
+        jnp.where(iota((count, count), 0) <= iota((count, count), 1), 1.0, 0.0).astype(bf16),
+        preferred_element_type=f32,
+    )[0:1]
+    keys_n = count + HALO
+    key = iota((1, keys_n), 1)
+    key = jnp.where(key < count, key, key - keys_n).astype(f32)
+    for r in range(byte_count // ROWS):
+        place = (iota((ROWS, 1), 0) + r * ROWS).astype(f32)
+        patch = jnp.sum(jnp.where(ends_row <= place, 1.0, 0.0), axis=1, keepdims=True)
+        floor = jnp.where(me == 0, jnp.maximum(patch - WIN, -1.0), patch - WIN)
+        bias[pl.ds(r * ROWS, ROWS)] = jnp.where((key <= patch) & (key > floor), 0.0, -1e30)
+
+    def attend(z, _=None):
+        square = jnp.sum(sq[...] + sq_in[...], axis=1, keepdims=True)
+        scale = lax.rsqrt(square / D + 1e-06)
+        low_half = iota((keys_n, 128), 1) < HEAD_DIM
+        for c in range(2):
+            slot = z * 2 + c
+            part_copy(slot).wait_recv()
+            kv[slot] = ((part[slot] + part_in[slot].astype(f32)) * scale).astype(bf16)
+            at = pl.ds(pl.multiple_of(slot * 128, 128), 128)
+            keys, values = kv[slot, :, pl.ds(0, 128)], kv[slot, :, pl.ds(128, 128)]
+
+            def chunk(r, carry):
+                rows = pl.ds(pl.multiple_of(r * ROWS, ROWS), ROWS)
+                q, shut = query[rows, at], bias[rows, :]
+                result = jnp.zeros((ROWS, 128), f32)
+                for low in (True, False):
+                    pick_head = low_half if low else jnp.logical_not(low_half)
+                    kh = jnp.where(pick_head, keys, jnp.zeros_like(keys))
+                    vh = jnp.where(pick_head, values, jnp.zeros_like(values))
+                    scores = lax.dot_general(q, kh, (((1,), (1,)), ((), ())), preferred_element_type=f32)
+                    scores = scores * (1.0 / math.sqrt(HEAD_DIM)) + shut
+                    expo = jnp.exp(scores - jnp.max(scores, axis=1, keepdims=True))
+                    weights = (expo / jnp.sum(expo, axis=1, keepdims=True)).astype(bf16)
+                    result = result + jnp.dot(weights, vh, preferred_element_type=f32)
+                att[rows, at] = result.astype(bf16)
+                return carry
+
+            lax.fori_loop(0, byte_count // ROWS, chunk, 0)
+
     arrive(1, 3)
     arrive_y(2, 2)
     local[5].wait()
@@ -357,78 +394,25 @@
     arrive_c(1, 1)
     arrive_c(2, 1)
     each(1, project)
+    sq_copy.wait_recv()
     arrive_c(1, 2)
     arrive_c(2, 2)
     arrive_y(2, 3)
     each(2, project)
+    attend(s)
+    each(1, attend)
     arrive_c(1, 3)
     arrive_c(2, 3)
     each(3, project)
-
-    ends_row = jnp.dot(
-        jnp.broadcast_to(lens_row.astype(f32), (8, count)).astype(bf16),
-        jnp.where(iota((count, count), 0) <= iota((count, count), 1), 1.0, 0.0).astype(bf16),
-        preferred_element_type=f32,
-    )[0:1]
-    sq_copy.wait_recv()
-    square = jnp.sum(sq[...] + sq_in[...], axis=1, keepdims=True)
-    scale = lax.rsqrt(square / D + 1e-06)
-
-    def finish(slot, carry):
-        part_copy(slot).wait_recv()
-        kv[slot] = ((part[slot] + part_in[slot].astype(f32)) * scale).astype(bf16)
-        return carry
-
-    lax.fori_loop(0, n, finish, 0)
+    each(2, attend)
+    each(3, attend)
     local[3].wait()
-    xc_copy(1).wait_recv()
-    keys_n = count + HALO
-    key = iota((1, keys_n), 1)
-    key = jnp.where(key < count, key, key - keys_n).astype(f32)
-    first = me == 0
-    low_half = iota((keys_n, 128), 1) < HEAD_DIM
-
-    def y_copy(r):
-        at = pl.ds(pl.multiple_of(t * half + r * ROWS, ROWS), ROWS)
-        return remote(y_out.at[pl.ds(r * ROWS, ROWS)], out_ref.at[at], y_send.at[r], y_recv.at[r], x_peer)
-
-    for r in range(half // ROWS):
-        place = (iota((ROWS, 1), 0) + (t * half + r * ROWS)).astype(f32)
-        patch = jnp.sum(jnp.where(ends_row <= place, 1.0, 0.0), axis=1, keepdims=True)
-        floor = jnp.where(first, jnp.maximum(patch - WIN, -1.0), patch - WIN)
-        bias = jnp.where((key <= patch) & (key > floor), 0.0, -1e30)
-
-        def heads(slot, carry):
-            at = pl.ds(pl.multiple_of(slot * 128, 128), 128)
-            q = query[pl.ds(r * ROWS, ROWS), at]
-            keys, values = kv[slot, :, pl.ds(0, 128)], kv[slot, :, pl.ds(128, 128)]
-            result = jnp.zeros((ROWS, 128), f32)
-            for low in (True, False):
-                pick_head = low_half if low else jnp.logical_not(low_half)
-                kh = jnp.where(pick_head, keys, jnp.zeros_like(keys))
-                vh = jnp.where(pick_head, values, jnp.zeros_like(values))
-                scores = lax.dot_general(q, kh, (((1,), (1,)), ((), ())), preferred_element_type=f32)
-                scores = scores * (1.0 / math.sqrt(HEAD_DIM)) + bias
-                expo = jnp.exp(scores - jnp.max(scores, axis=1, keepdims=True))
-                weights = (expo / jnp.sum(expo, axis=1, keepdims=True)).astype(bf16)
-                result = result + jnp.dot(weights, vh, preferred_element_type=f32)
-            att[pl.ds(r * ROWS, ROWS), at] = result.astype(bf16)
-            return carry
-
-        lax.fori_loop(0, n, heads, 0)
-        at = pl.ds(pl.multiple_of(t * half + r * ROWS, ROWS), ROWS)
-        a = att[pl.ds(r * ROWS, ROWS), :]
-        for who in (1 - t, t):
-            at_cols = pl.ds(pl.multiple_of(who * cols, cols), cols)
-            value = br[at, at_cols].astype(f32) + jnp.dot(a, wo[who], preferred_element_type=f32)
-            if who is t:
-                out_ref[at, :] = value.astype(bf16)
-            else:
-                y_out[pl.ds(r * ROWS, ROWS), :] = value.astype(bf16)
-                y_copy(r).start()
-
-    for r in range(half // ROWS):
-        y_copy(r).wait()
+    my_cols = pl.ds(pl.multiple_of(t * cols, cols), cols)
+    for r in range(byte_count // ROWS):
+        rows = pl.ds(r * ROWS, ROWS)
+        value = br[rows, my_cols].astype(f32) + jnp.dot(att[rows, :], wo[...], preferred_element_type=f32)
+        out_ref[rows, :] = value.astype(bf16)
+
     for kind in range(3):
         pl.when(s + 1 < n_seq)(lambda: right(kind, s, True).wait_send())
         pl.when(s > 0)(lambda: left(kind, s, True).wait_send())
@@ -446,9 +430,8 @@
             each(k, sent)
     for i in range(1, n):
         stream_copy(i).wait_send()
-    for i in range(2):
-        x_copy(i).wait_send()
-        xc_copy(i).wait_send()
+    x_copy(0).wait_send()
+    xc_copy(0).wait_send()
     halo_pooled.wait_send()
     halo_stream.wait_send()
     sq_copy.wait_send()
@@ -464,9 +447,7 @@
     count = patch_owner.shape[0]
     depth, width = w_in.shape
     cols = w_query.shape[1]
-    half = byte_count // 2
     tall = count + HALO
-    chunks = half // ROWS
     any_spec, vmem = pl.BlockSpec(memory_space=pl.ANY), pl.BlockSpec(memory_space=pltpu.VMEM)
     dma = pltpu.SemaphoreType.DMA
     return pl.pallas_call(
@@ -480,7 +461,7 @@
             pltpu.VMEM(patch_stream.shape, bf16),
             pltpu.VMEM((byte_count, dl), bf16),
             pltpu.VMEM((2, dl, cols), bf16),
-            pltpu.VMEM((2, dl, cols), bf16),
+            pltpu.VMEM((dl, cols), bf16),
             pltpu.VMEM((tall, dl), bf16),
             pltpu.VMEM((tall, width), f32),
             pltpu.VMEM((tall, width), bf16),
@@ -492,9 +473,9 @@
             pltpu.VMEM((n, tall, 256), bf16),
             pltpu.VMEM((tall, 128), f32),
             pltpu.VMEM((tall, 128), f32),
-            pltpu.VMEM((half, dl), bf16),
-            pltpu.VMEM((half, dl), bf16),
-            pltpu.VMEM((half, cols), bf16),
+            pltpu.VMEM((byte_count, dl), bf16),
+            pltpu.VMEM((byte_count, dl), bf16),
+            pltpu.VMEM((byte_count, tall), f32),
             dma((3, n, 2)),
             dma((3, n_seq)),
             dma((3, n_seq)),
@@ -511,8 +492,6 @@
             dma((2,)),
             dma((n + 1,)),
             dma((n + 1,)),
-            dma((chunks,)),
-            dma((chunks,)),
         ],
         compiler_params=pltpu.CompilerParams(
             collective_id=0, has_side_effects=True, vmem_limit_bytes=56 * 1024 * 1024

time: 124 us -> 119 us (0.960)
  Pallas kernels: 120 us -> 115 us
    pallas_call x1, Pallas kernels: 120 us -> 115 us  [fused(): pl.pallas_call(functools.partial(fused_kernel, n_seq), out_shape=jax.Shap...]
where the time goes in v3:
time: 119 us
  Pallas kernels  115 us (97%)
  local copies, waits for them, and re-layouts  3.65 us (3%)
    pallas_call x1, Pallas kernels, fused(): pl.pallas_call(functools.partial(fused_kernel, n_seq), out_shape=jax.Shap...  115 us
    unnamed x2, local copies, waits for them, and re-layouts  3.65 us

profile of v3, /device:TPU:0, one launch (start us, length us, event | category | flops | bytes accessed | tf_op | source)
XLA Modules:
  0.0 118.8 jit_solution(8885631939767129595)
XLA Ops:
  0.0 1.4 %copy.10.own_col_ref = s32[128,1]{1,0:T(8,128)} copy(s32[128,1]{0,1:T(1,128)} %param.11) | data formatting | bytes 1024 | tf_op args[2]
  1.4 115.1 %shard_map.91 = bf16[1024,512]{1,0:T(8,128)(2,1)} custom-call(bf16[1024,1024]{1,0:T(8,128)(2,1)} %rows_ref.1, s32[1,128]{1,0:T(1,128)} %lens_ref.1, s32[128,1]{1,0:T(8,128)} %copy.10.own_col_ref, s32[1,128]{1,0:T(1,128)} %bitcast.2, bf16[256,2048]{1,0:T(8,128)(2,1)} %stream_ref.1, bf16[128,2048]{1,0:T(8,128)(2,1)} %w_in_ref.1, f32[1,2048]{1,0:T(1,128)} %bitcast.3, ...), custom_call_target="tpu_custom_call" | custom-call | flops 8999999488 | bytes 8000000 | tf_op jit(solution)/shard_map/pallas_call | solution.py:453
  116.5 2.3 %copy.12 = bf16[1024,512]{1,0:T(8,128)(2,1)} copy(bf16[1024,512]{1,0:T(8,128)(2,1)} %shard_map.91) | data formatting | bytes 2097152

commit v4 on v3

--- a/solution.py
+++ b/solution.py
@@ -287,7 +287,7 @@
     for part_t in range(2):
         query[:, part_t * cols:(part_t + 1) * cols] = jnp.dot(
             br[...], wq[part_t], preferred_element_type=f32
-        ).astype(bf16)
+        ).astype(bf16) * (1.0 / math.sqrt(HEAD_DIM))
     arrive_y(1, 1)
     arrive(1, 2)
     arrive_y(2, 1)
@@ -374,9 +374,9 @@
                     kh = jnp.where(pick_head, keys, jnp.zeros_like(keys))
                     vh = jnp.where(pick_head, values, jnp.zeros_like(values))
                     scores = lax.dot_general(q, kh, (((1,), (1,)), ((), ())), preferred_element_type=f32)
-                    scores = scores * (1.0 / math.sqrt(HEAD_DIM)) + shut
+                    scores = scores + shut
                     expo = jnp.exp(scores - jnp.max(scores, axis=1, keepdims=True))
-                    weights = (expo / jnp.sum(expo, axis=1, keepdims=True)).astype(bf16)
+                    weights = (expo * (1.0 / jnp.sum(expo, axis=1, keepdims=True))).astype(bf16)
                     result = result + jnp.dot(weights, vh, preferred_element_type=f32)
                 att[rows, at] = result.astype(bf16)
                 return carry

time: 119 us -> 119 us (level)
  no operation moved by 1% of the time
where the time goes in v4:
time: 119 us
  Pallas kernels  115 us (97%)
  local copies, waits for them, and re-layouts  3.65 us (3%)
    pallas_call x1, Pallas kernels, fused(): pl.pallas_call(functools.partial(fused_kernel, n_seq), out_shape=jax.Shap...  115 us
    unnamed x2, local copies, waits for them, and re-layouts  3.65 us

profile of v4, /device:TPU:0, one launch (start us, length us, event | category | flops | bytes accessed | tf_op | source)
XLA Modules:
  0.0 118.8 jit_solution(16368743510066956553)
XLA Ops:
  0.0 1.4 %copy.10.own_col_ref = s32[128,1]{1,0:T(8,128)} copy(s32[128,1]{0,1:T(1,128)} %param.11) | data formatting | bytes 1024 | tf_op args[2]
  1.4 115.1 %shard_map.91 = bf16[1024,512]{1,0:T(8,128)(2,1)} custom-call(bf16[1024,1024]{1,0:T(8,128)(2,1)} %rows_ref.1, s32[1,128]{1,0:T(1,128)} %lens_ref.1, s32[128,1]{1,0:T(8,128)} %copy.10.own_col_ref, s32[1,128]{1,0:T(1,128)} %bitcast.2, bf16[256,2048]{1,0:T(8,128)(2,1)} %stream_ref.1, bf16[128,2048]{1,0:T(8,128)(2,1)} %w_in_ref.1, f32[1,2048]{1,0:T(1,128)} %bitcast.3, ...), custom_call_target="tpu_custom_call" | custom-call | flops 8999999488 | bytes 8000000 | tf_op jit(solution)/shard_map/pallas_call | solution.py:453
  116.5 2.3 %copy.12 = bf16[1024,512]{1,0:T(8,128)(2,1)} copy(bf16[1024,512]{1,0:T(8,128)(2,1)} %shard_map.91) | data formatting | bytes 2097152
